TPU v7x, 32 devices: a whole 2x2x4 slice. The times are simulated.
32 devices in a mesh: row: 4 (over y, core), col: 8 (over z, x).
Axes of the slice: x: 2, y: 2, z: 4, core: 2. Of those that a mesh axis runs over, the one named last changes fastest.
Arguments:
- left: bfloat16 [8, 16, 512, 256], P('row', 'col'), may hold values from -0.11767578 to 0.11767578
- right: bfloat16 [8, 16, 512, 256], P('row', 'col'), may hold values from -6 to 6
- lower_inverse: bfloat16 [2, 512, 512], P(None, 'row'), as said below
- upper_inverse: bfloat16 [2, 512, 512], P(None, None, 'col'), as said below
- ranks: int32 [8, 16], P('row', 'col'), may hold values from 16 to 256, as said below
Outputs:
- right_out: bfloat16 [8, 16, 512, 256], P('row', 'col')
Inputs may be any that keep to these rules, and one draw needn't show every extreme that they name: Tile ranks: every row of `ranks` contains at least one entry equal to 256; all entries lie in 4..256. Each lower_inverse[k] is lower triangular with a positive diagonal. Each upper_inverse[k] is upper triangular with a positive diagonal.
All inputs are finite; a program needn't handle non-finite values.
Results may differ from a plain program's by a relative error of at most 0.009.
Values may be sent and summed in bfloat16 or wider, within the bound.
A program may use at most 64 MiB of HBM per device.

v0:
```python
import functools

import jax
import jax.numpy as jnp
from jax import lax
from jax.experimental import pallas as pl
from jax.experimental.pallas import tpu as pltpu
from jax.sharding import PartitionSpec as P

CHUNKS = 4
MESH = pl.DeviceIdType.MESH


def matmul(a, b):
    return jnp.dot(a, b, preferred_element_type=jnp.float32)


def matmul_tn(a, b):
    return lax.dot_general(a, b, (((0,), (0,)), ((), ())), preferred_element_type=jnp.float32)


def matmul_nt(a, b):
    return lax.dot_general(a, b, (((1,), (1,)), ((), ())), preferred_element_type=jnp.float32)


def children(index, extent, minor, source):
    x, m = lax.rem(index, minor), lax.div(index, minor)
    found = [((x == source) & (m + 1 < extent // minor), index + minor)]
    if source + 1 < minor:
        found.append(((x >= source) & (x + 1 < minor), index + 1))
    if source > 0:
        found.append(((x <= source) & (x >= 1), index - 1))
    return found


def kernel(
    n_row, n_col, minor_col, ranks, left, right, lower, upper, out,
    ul, col_u, col_y, row_y, row_u, low, up,
    send_sem, recv_sem, inv_send, low_recv, up_recv, fetch_sem, swap_sem,
):
    r, c = lax.axis_index("row"), lax.axis_index("col")
    order, width = left.shape[2], left.shape[3]
    step = order // CHUNKS
    fetch_left = [
        [pltpu.make_async_copy(left.at[a, b], ul.at[a, b], fetch_sem.at[0, a, b]) for b in range(2)]
        for a in range(2)
    ]
    fetch_right = [
        [pltpu.make_async_copy(right.at[a, b], out.at[a, b], fetch_sem.at[1, a, b]) for b in range(2)]
        for a in range(2)
    ]
    every = [(1, 0), (0, 0), (0, 1), (1, 1)]
    for a, b in every:
        fetch_left[a][b].start()
    for a, b in every:
        fetch_right[a][b].start()

    barrier = pltpu.get_barrier_semaphore()
    for d in range(1, n_row):
        pl.semaphore_signal(
            barrier, inc=1, device_id={"row": lax.rem(r + d, n_row)}, device_id_type=MESH
        )
    for d in range(1, n_col):
        pl.semaphore_signal(
            barrier, inc=1, device_id={"col": lax.rem(c + d, n_col)}, device_id_type=MESH
        )

    own_rows = {"up": upper.shape[1], "low": lower.shape[1]}

    def own_up(k):
        rows = own_rows["up"]
        half = pl.ds(pl.multiple_of(lax.rem(r, 2) * (order // 2), order // 2), order // 2)
        return pltpu.make_async_copy(
            upper.at[k, :, half], up.at[pl.ds(k * rows, rows), half], inv_send.at[0, k]
        )

    def own_low(k):
        rows = own_rows["low"]
        return pltpu.make_async_copy(lower.at[k], low.at[pl.ds(k * rows, rows)], inv_send.at[1, k])

    for k in range(2):

        @pl.when(c == k)
        def _():
            own_up(k).start()

        @pl.when(r == k)
        def _():
            own_low(k).start()

    lanes = lax.broadcasted_iota(jnp.int32, (1, width), 1)

    def keep(a, b):
        return (lanes < ranks[a, b]).astype(jnp.float32).astype(jnp.bfloat16)

    buffers = {"cu": col_u, "cy": col_y, "ru": row_u, "ry": row_y}
    place = {
        (kind, k, t): n
        for n, (kind, k, t) in enumerate(
            (kind, k, t) for kind in ("cu", "cy", "ru", "ry") for k in range(2) for t in range(2)
        )
    }

    def axis_of(item):
        return "col" if item[0][0] == "c" else "row"

    def tree(item):
        if axis_of(item) == "col":
            return children(c, n_col, minor_col, item[1])
        return children(r, n_row, 2, item[1])

    def copy_of(item, chunk, way, target):
        kind, k, t = item
        view = buffers[kind].at[k, t, pl.ds(chunk * step, step)]
        return pltpu.make_async_remote_copy(
            src_ref=view,
            dst_ref=view,
            send_sem=send_sem.at[place[item], chunk, way],
            recv_sem=recv_sem.at[place[item], chunk],
            device_id={axis_of(item): target},
            device_id_type=MESH,
        )

    def wanted(item):
        kind, k, t = item
        if t > 0:
            return True
        return (r if axis_of(item) == "col" else c) > k

    def is_source(item):
        return (c if axis_of(item) == "col" else r) == item[1]

    def is_main(item):
        if axis_of(item) == "col":
            return lax.rem(c, minor_col) == item[1]
        return lax.rem(r, 2) == item[1]

    def forward(item, chunk):
        for way, (needed, target) in enumerate(tree(item)):

            @pl.when(needed)
            def _():
                copy_of(item, chunk, way, target).start()

    def send(item, also=True):
        @pl.when(is_source(item) & wanted(item) & also)
        def _():
            for chunk in range(CHUNKS):
                forward(item, chunk)

    def relay(items, also=True, chunks=range(CHUNKS)):
        for chunk in chunks:
            for item, main in items:
                role = is_main(item) if main else jnp.logical_not(is_main(item))

                @pl.when(jnp.logical_not(is_source(item)) & wanted(item) & role & also)
                def _():
                    copy_of(item, chunk, 0, 0).wait_recv()
                    forward(item, chunk)

    def main(*items, also=True):
        relay([(item, True) for item in items], also)

    def leaf(*items, also=True):
        relay([(item, False) for item in items], also)

    half = order // 2
    mine = pl.ds(pl.multiple_of(lax.rem(r, 2) * half, half), half)

    def swap_halves():
        return pltpu.make_async_remote_copy(
            src_ref=up.at[:, mine],
            dst_ref=up.at[:, mine],
            send_sem=swap_sem.at[0],
            recv_sem=swap_sem.at[1],
            device_id={"row": r + 1 - 2 * lax.rem(r, 2)},
            device_id_type=MESH,
        )

    def up_copy(k, source):
        rows = upper.shape[1]
        return pltpu.make_async_remote_copy(
            src_ref=upper.at[k, :, mine],
            dst_ref=up.at[pl.ds(pl.multiple_of(source * rows, rows), rows), mine],
            send_sem=inv_send.at[0, k],
            recv_sem=up_recv.at[source],
            device_id={"col": k},
            device_id_type=MESH,
        )

    def low_copy(k, source):
        rows = lower.shape[1]
        return pltpu.make_async_remote_copy(
            src_ref=lower.at[k],
            dst_ref=low.at[pl.ds(pl.multiple_of(source * rows, rows), rows)],
            send_sem=inv_send.at[1, k],
            recv_sem=low_recv.at[source],
            device_id={"row": k},
            device_id_type=MESH,
        )

    for a in range(2):
        fetch_left[a][0].wait()
        ul[a, 0] = ul[a, 0] * keep(a, 0)
        for k in range(2):

            @pl.when(c == k)
            def _():
                col_u[k, a] = ul[a, 0]

    pl.semaphore_wait(barrier, n_row - 1 + n_col - 1)

    for k in range(2):

        @pl.when(c != k)
        def _():
            up_copy(k, c).start()

        @pl.when(r != k)
        def _():
            low_copy(k, r).start()

    send(("cu", 0, 0))
    send(("cu", 0, 1), also=r >= 2)
    send(("cu", 1, 0))
    send(("cu", 1, 1))
    for a, b in ((0, 0), (0, 1), (1, 0), (1, 1)):
        fetch_right[a][b].wait()
        out[a, b] = out[a, b] * keep(a, b)
        if a == 0:

            @pl.when(r == 0)
            def _():
                row_y[0, b] = out[0, b]

            send(("ry", 0, b))
    for a, b in ((0, 1), (1, 1)):
        fetch_left[a][b].wait()
        ul[a, b] = ul[a, b] * keep(a, b)

    for k in range(2):

        @pl.when(c == k)
        def _():
            own_up(k).wait()

        @pl.when(r == k)
        def _():
            own_low(k).wait()

    @pl.when(c < 2)
    def _():
        for s in range(n_col):

            @pl.when(s != c)
            def _():
                up_copy(0, s).wait_recv()

        swap_halves().start()
        swap_halves().wait_recv()

    @pl.when(c == 0)
    def _():
        col_y[0, 0] = matmul(up[...], out[0, 0]).astype(jnp.bfloat16)

    send(("cy", 0, 0))
    send(("cu", 0, 1), also=r < 2)

    @pl.when(c == 0)
    def _():
        col_y[0, 1] = matmul(up[...], out[1, 0]).astype(jnp.bfloat16)

    send(("cy", 0, 1))

    @pl.when(r < 2)
    def _():
        for s in range(n_row):

            @pl.when(s != r)
            def _():
                low_copy(0, s).wait_recv()

    for b in range(2):
        for k in range(2):

            @pl.when(r == k)
            def _():
                row_u[k, b] = matmul(low[...], ul[0, b]).astype(jnp.bfloat16)

            send(("ru", k, b))

    def update(panel, a, b, also=True):
        row_in = (a * n_row + r) > panel
        tile_col = b * n_col + c

        @pl.when(row_in & (tile_col > panel) & also)
        def _():
            core = matmul_tn(col_y[panel, a], row_u[panel, b]).astype(jnp.bfloat16)
            meet = matmul_tn(ul[a, b], col_u[panel, a]).astype(jnp.bfloat16)
            mixed = matmul(meet, core).astype(jnp.bfloat16)
            change = matmul_nt(row_y[panel, b], mixed)
            out[a, b] = (out[a, b].astype(jnp.float32) - change).astype(jnp.bfloat16)

        if b == 0:

            @pl.when(row_in & (c == panel) & also)
            def _():
                out[a, 0] = col_y[panel, a]

    def solve_next(a):
        @pl.when(c == 1)
        def _():
            col_y[1, a] = matmul(up[...], out[a, 0]).astype(jnp.bfloat16)

        send(("cy", 1, a))

    def share_row(b):
        @pl.when(r == 1)
        def _():
            row_y[1, b] = out[0, b]

        send(("ry", 1, b))

    main(("cu", 0, 0), ("cu", 1, 0), ("ry", 0, 0))
    main(("cy", 0, 0), also=r < 2)
    leaf(("cu", 0, 0), ("ry", 0, 0), ("cy", 0, 0), ("ru", 0, 0), also=r == 1)
    update(0, 0, 0, also=r == 1)
    share_row(0)
    leaf(("ry", 0, 1), ("ru", 0, 1), also=r == 1)
    update(0, 0, 1, also=r == 1)
    share_row(1)
    main(("cu", 0, 1), ("cu", 1, 1), ("ry", 0, 1))
    main(("cy", 0, 0), ("ru", 0, 0), also=r >= 2)
    main(("ru", 1, 0))
    leaf(("cu", 0, 0), ("ry", 0, 0), ("cy", 0, 0), ("ru", 0, 0), also=r != 1)
    update(0, 0, 0, also=r != 1)
    solve_next(0)
    main(("cy", 0, 1), ("cy", 1, 0), ("ru", 0, 1), ("ru", 1, 1))
    leaf(("cu", 0, 1))
    leaf(("cy", 0, 1))
    update(0, 1, 0, also=c == 1)
    solve_next(1)
    leaf(("ry", 0, 1), ("ru", 0, 1), also=r != 1)
    quarter = CHUNKS // 4
    last = [range(quarter * n, quarter * (n + 1)) for n in range(4)]
    relay([(("cy", 1, 1), True)], chunks=last[0])
    update(0, 1, 0, also=c != 1)
    relay([(("cy", 1, 1), True)], chunks=last[1])
    update(0, 0, 1, also=r != 1)
    relay([(("cy", 1, 1), True)], chunks=last[2])
    update(0, 1, 1)
    relay([(("cy", 1, 1), True)], chunks=last[3])
    main(("ry", 1, 0))
    main(("ry", 1, 1))
    leaf(("cu", 1, 0), ("cy", 1, 0), ("ru", 1, 0), ("ry", 1, 0))
    update(1, 0, 0)
    leaf(("ru", 1, 1), ("ry", 1, 1), ("cu", 1, 1))
    update(1, 0, 1)
    leaf(("cy", 1, 1))
    update(1, 1, 0)
    update(1, 1, 1)

    for k in range(2):

        @pl.when(c != k)
        def _():
            up_copy(k, c).wait_send()

        @pl.when(r != k)
        def _():
            low_copy(k, r).wait_send()

    @pl.when(c < 2)
    def _():
        swap_halves().wait_send()

    for item in place:
        for way, (needed, target) in enumerate(tree(item)):

            @pl.when(needed & wanted(item))
            def _():
                for chunk in range(CHUNKS):
                    copy_of(item, chunk, way, target).wait_send()


def body(left, right, lower_inverse, upper_inverse, ranks):
    n_row, n_col = lax.axis_size("row"), lax.axis_size("col")
    minor_col = 4 if n_col % 4 == 0 and n_col > 8 else 2
    order, width = left.shape[2:]
    upper = jnp.swapaxes(upper_inverse, 1, 2)
    tile = (order, width)
    vmem = pl.BlockSpec(memory_space=pltpu.VMEM)
    hbm = pl.BlockSpec(memory_space=pltpu.HBM)
    return pl.pallas_call(
        functools.partial(kernel, n_row, n_col, minor_col),
        out_shape=jax.ShapeDtypeStruct(right.shape, jnp.bfloat16),
        in_specs=[pl.BlockSpec(memory_space=pltpu.SMEM)] + [hbm] * 4,
        out_specs=vmem,
        scratch_shapes=[
            pltpu.VMEM((2, 2) + tile, jnp.bfloat16),
            pltpu.VMEM((2, 2) + tile, jnp.bfloat16),
            pltpu.VMEM((2, 2) + tile, jnp.bfloat16),
            pltpu.VMEM((2, 2) + tile, jnp.bfloat16),
            pltpu.VMEM((2, 2) + tile, jnp.bfloat16),
            pltpu.VMEM((order, order), jnp.bfloat16),
            pltpu.VMEM((order, order), jnp.bfloat16),
            pltpu.SemaphoreType.DMA((16, CHUNKS, 3)),
            pltpu.SemaphoreType.DMA((16, CHUNKS)),
            pltpu.SemaphoreType.DMA((2, 2)),
            pltpu.SemaphoreType.DMA((n_row,)),
            pltpu.SemaphoreType.DMA((n_col,)),
            pltpu.SemaphoreType.DMA((2, 2, 2)),
            pltpu.SemaphoreType.DMA((2,)),
        ],
        compiler_params=pltpu.CompilerParams(
            collective_id=0, has_side_effects=True, vmem_limit_bytes=60 * 1024 * 1024
        ),
        cost_estimate=pl.CostEstimate(
            flops=2_000_000_000, bytes_accessed=4_000_000, transcendentals=0
        ),
    )(ranks, left, right, lower_inverse, upper)


def solution(mesh):
    placed = (
        P("row", "col", None, None),
        P("row", "col", None, None),
        P(None, "row", None),
        P(None, None, "col"),
        P("row", "col"),
    )
    return jax.shard_map(
        body, mesh=mesh, in_specs=placed, out_specs=P("row", "col", None, None), check_vma=False
    )
```

profile of v0, /device:TPU:28, one launch (start us, length us, event | category | flops | bytes accessed | tf_op | source)
XLA Modules:
  0.0 55.9 jit_solution(14675373165151027733)
XLA Ops:
  0.0 53.6 %shard_map.55 = bf16[2,2,512,256]{3,2,1,0:T(8,128)(2,1)} custom-call(s32[2,2]{1,0:T(2,128)} %ranks.1, bf16[2,2,512,256]{3,2,1,0:T(8,128)(2,1)} %left.1, bf16[2,2,512,256]{3,2,1,0:T(8,128)(2,1)} %right.1, bf16[2,128,512]{2,1,0:T(8,128)(2,1)} %lower.1, bf16[2,64,512]{2,1,0:T(8,128)(2,1)} %bitcast.1), custom_call_target="tpu_custom_call" | custom-call | flops 2000000000 | bytes 4000000 | tf_op jit(solution)/shard_map/pallas_call | solution.py:394
  53.6 2.3 %copy.7 = bf16[2,2,512,256]{3,2,1,0:T(8,128)(2,1)} copy(bf16[2,2,512,256]{3,2,1,0:T(8,128)(2,1)} %shard_map.55) | data formatting | bytes 2097152
where the time goes:
time: 56.1 us; the launch traced here: 55.9 us
  Pallas kernels  53.6 us (96%)
  local copies, waits for them, and re-layouts  2.26 us (4%)
    pallas_call x1, Pallas kernels, body(): pl.pallas_call(functools.partial(kernel, n_row, n_col, minor_col), out_sh...  53.6 us
    unnamed x1, local copies, waits for them, and re-layouts  2.26 us

commit v1 on v0

--- a/solution.py
+++ b/solution.py
@@ -56,14 +56,28 @@
         fetch_right[a][b].start()
 
     barrier = pltpu.get_barrier_semaphore()
+
+    def greet(needed, **target):
+        @pl.when(needed)
+        def _():
+            pl.semaphore_signal(barrier, inc=1, device_id=target, device_id_type=MESH)
+
+    def count(*needed):
+        return sum(flag.astype(jnp.int32) for flag in needed)
+
+    x = lax.rem(c, minor_col)
+    greet(r >= 2, row=r - 2)
+    greet(r >= 0, row=r + 1 - 2 * lax.rem(r, 2))
+    greet(x + 1 < minor_col, col=c + 1)
+    greet(x >= 1, col=c - 1)
+    greet(c >= minor_col, col=c - minor_col)
     for d in range(1, n_row):
-        pl.semaphore_signal(
-            barrier, inc=1, device_id={"row": lax.rem(r + d, n_row)}, device_id_type=MESH
-        )
+        greet(r < 2, row=lax.rem(r + d, n_row))
     for d in range(1, n_col):
-        pl.semaphore_signal(
-            barrier, inc=1, device_id={"col": lax.rem(c + d, n_col)}, device_id_type=MESH
-        )
+        greet(c < 2, col=lax.rem(c + d, n_col))
+    greeted = 1 + count(
+        r + 2 < n_row, x + 1 < minor_col, x >= 1, c + minor_col < n_col, r != 0, r != 1, c != 0, c != 1
+    )
 
     own_rows = {"up": upper.shape[1], "low": lower.shape[1]}
 
@@ -208,7 +222,7 @@
             def _():
                 col_u[k, a] = ul[a, 0]
 
-    pl.semaphore_wait(barrier, n_row - 1 + n_col - 1)
+    pl.semaphore_wait(barrier, greeted)
 
     for k in range(2):
 

time: 56.1 us -> 53.4 us (0.952)
  Pallas kernels: 53.6 us -> 50.9 us
    pallas_call x1, Pallas kernels: 53.6 us -> 50.9 us  [body(): pl.pallas_call(functools.partial(kernel, n_row, n_col, minor_col), out_sh...]
where the time goes in v1:
time: 53.4 us; the launch traced here: 53.2 us
  Pallas kernels  50.9 us (95%)
  local copies, waits for them, and re-layouts  2.26 us (4%)
    pallas_call x1, Pallas kernels, body(): pl.pallas_call(functools.partial(kernel, n_row, n_col, minor_col), out_sh...  50.9 us
    unnamed x1, local copies, waits for them, and re-layouts  2.26 us

profile of v1, /device:TPU:28, one launch (start us, length us, event | category | flops | bytes accessed | tf_op | source)
XLA Modules:
  0.0 53.2 jit_solution(11761498729298996597)
XLA Ops:
  0.0 50.9 %shard_map.55 = bf16[2,2,512,256]{3,2,1,0:T(8,128)(2,1)} custom-call(s32[2,2]{1,0:T(2,128)} %ranks.1, bf16[2,2,512,256]{3,2,1,0:T(8,128)(2,1)} %left.1, bf16[2,2,512,256]{3,2,1,0:T(8,128)(2,1)} %right.1, bf16[2,128,512]{2,1,0:T(8,128)(2,1)} %lower.1, bf16[2,64,512]{2,1,0:T(8,128)(2,1)} %bitcast.1), custom_call_target="tpu_custom_call" | custom-call | flops 2000000000 | bytes 4000000 | tf_op jit(solution)/shard_map/pallas_call | solution.py:408
  50.9 2.3 %copy.7 = bf16[2,2,512,256]{3,2,1,0:T(8,128)(2,1)} copy(bf16[2,2,512,256]{3,2,1,0:T(8,128)(2,1)} %shard_map.55) | data formatting | bytes 2097152

commit v2 on v1

v2 whole, which is shorter than its diff:
```python
import functools

import jax
import jax.numpy as jnp
from jax import lax
from jax.experimental import pallas as pl
from jax.experimental.pallas import tpu as pltpu
from jax.sharding import PartitionSpec as P

CHUNKS = 8
MESH = pl.DeviceIdType.MESH


def matmul(a, b):
    return jnp.dot(a, b, preferred_element_type=jnp.float32)


def matmul_tn(a, b):
    return lax.dot_general(a, b, (((0,), (0,)), ((), ())), preferred_element_type=jnp.float32)


def matmul_nt(a, b):
    return lax.dot_general(a, b, (((1,), (1,)), ((), ())), preferred_element_type=jnp.float32)


def kernel(
    n_row, n_col, minor_col, ranks, left, right, lower, upper, out,
    ul, colb, rowb, low, up, mix,
    col_send, col_recv, row_send, row_recv, inv_send, low_recv, up_recv, fetch_sem, swap_sem, extra_sem,
):
    r, c = lax.axis_index("row"), lax.axis_index("col")
    x, core = lax.rem(c, minor_col), lax.rem(r, 2)
    order, width = left.shape[2], left.shape[3]
    step = order // CHUNKS
    fetch_left = [
        [pltpu.make_async_copy(left.at[a, b], ul.at[a, b], fetch_sem.at[0, a, b]) for b in range(2)]
        for a in range(2)
    ]
    fetch_right = [
        [pltpu.make_async_copy(right.at[a, b], out.at[a, b], fetch_sem.at[1, a, b]) for b in range(2)]
        for a in range(2)
    ]
    every = [(0, 0), (1, 0), (0, 1), (1, 1)]
    for a, b in every:
        fetch_left[a][b].start()
    for a, b in every:
        fetch_right[a][b].start()

    barrier = pltpu.get_barrier_semaphore()

    def greet(needed, **target):
        @pl.when(needed)
        def _():
            pl.semaphore_signal(barrier, inc=1, device_id=target, device_id_type=MESH)

    def count(*needed):
        return sum(flag.astype(jnp.int32) for flag in needed)

    greet(c >= minor_col, col=c - minor_col)
    greet(r >= 2, row=r - 2)
    greet(r >= 0, row=r + 1 - 2 * core)
    greet(x + 1 < minor_col, col=c + 1)
    greet(x >= 1, col=c - 1)
    for d in range(1, n_row):
        greet(r < 2, row=lax.rem(r + d, n_row))
    for d in range(1, n_col):
        greet(c < 2, col=lax.rem(c + d, n_col))
    greeted = 1 + count(
        r + 2 < n_row, x + 1 < minor_col, x >= 1, c + minor_col < n_col, r != 0, r != 1, c != 0, c != 1
    )

    half = order // 2
    mine = pl.ds(pl.multiple_of(core * half, half), half)
    up_rows, low_rows = upper.shape[1], lower.shape[1]

    def own_up(k):
        return pltpu.make_async_copy(
            upper.at[k, :, mine], up.at[pl.ds(k * up_rows, up_rows), mine], inv_send.at[0, k]
        )

    def own_low(k):
        return pltpu.make_async_copy(
            lower.at[k], low.at[pl.ds(k * low_rows, low_rows)], inv_send.at[1, k]
        )

    for k in range(2):

        @pl.when(c == k)
        def _():
            own_up(k).start()

        @pl.when(r == k)
        def _():
            own_low(k).start()

    lanes = lax.broadcasted_iota(jnp.int32, (1, width), 1)

    def keep(a, b):
        return (lanes < ranks[a, b]).astype(jnp.float32).astype(jnp.bfloat16)

    def col_slot(kind, k, t):
        return 2 * t + kind if k == 0 else 2 * kind + t

    def row_slot(kind, k, t):
        return 2 * (1 - kind) + t if k == 0 else 2 * kind + t

    def col_wanted(k, slot):
        t = slot // 2 if k == 0 else slot % 2
        return True if t > 0 else r > k

    def row_wanted(k, slot):
        return True if slot % 2 > 0 or (k, slot) == (0, 2) else c > k

    def piece(q):
        return pl.ds(pl.multiple_of(q * step, step), step)

    def col_copy(k, slot, q, way, target):
        view = colb.at[k, slot] if q is None else colb.at[k, slot, piece(q)]
        return pltpu.make_async_remote_copy(
            src_ref=view,
            dst_ref=view,
            send_sem=col_send.at[k, slot, way],
            recv_sem=col_recv.at[k, slot, 0 if q is None else q],
            device_id={"col": target},
            device_id_type=MESH,
        )

    def row_copy(k, slot, q, way, target):
        view = rowb.at[k, slot] if q is None else rowb.at[k, slot, piece(q)]
        return pltpu.make_async_remote_copy(
            src_ref=view,
            dst_ref=view,
            send_sem=row_send.at[k, slot, way],
            recv_sem=row_recv.at[k, slot, 0 if q is None else q],
            device_id={"row": target},
            device_id_type=MESH,
        )

    def col_ways(k):
        return [
            ((x == k) & (c + minor_col < n_col), c + minor_col),
            ((x >= k) & (x + 1 < minor_col), c + 1),
            ((x <= k) & (x >= 1), c - 1),
        ]

    def row_ways():
        return [(r + 2 < n_row, r + 2), (r >= 0, r + 1 - 2 * core)]

    def col_forward(k, slot, q, ways=(0, 1, 2)):
        for way in ways:
            needed, target = col_ways(k)[way]

            @pl.when(needed)
            def _():
                col_copy(k, slot, q, way, target).start()

    def row_forward(k, slot, q):
        for way, (needed, target) in enumerate(row_ways()):

            @pl.when(needed)
            def _():
                row_copy(k, slot, q, way, target).start()

    def col_send_out(k, slot, ways=(0, 1, 2)):
        @pl.when((c == k) & col_wanted(k, slot))
        def _():
            @pl.loop(0, CHUNKS)
            def _(q):
                col_forward(k, slot, q, ways)

    def row_send_out(k, slot):
        @pl.when((r == k) & row_wanted(k, slot))
        def _():
            @pl.loop(0, CHUNKS)
            def _(q):
                row_forward(k, slot, q)

    trunk = jnp.minimum(x, 1)

    def col_relay_piece(slot, q):
        col_copy(trunk, slot, q, 0, 0).wait_recv()
        col_forward(trunk, slot, q)

    def col_relay(slot, also):
        @pl.when((c >= 2) & (x < 2) & also)
        def _():
            @pl.loop(0, CHUNKS)
            def _(q):
                col_relay_piece(slot, q)

    def row_relay_piece(slot, q):
        row_copy(core, slot, q, 0, 0).wait_recv()
        row_forward(core, slot, q)

    def row_relay(slot, also):
        @pl.when((r >= 2) & also)
        def _():
            @pl.loop(0, CHUNKS)
            def _(q):
                row_relay_piece(slot, q)

    def col_leaf(k, *slots, also=True):
        for slot in slots:

            @pl.when((x != k) & col_wanted(k, slot) & also)
            def _():
                @pl.loop(0, CHUNKS)
                def _(q):
                    col_copy(k, slot, q, 0, 0).wait_recv()
                    if minor_col > 2:
                        col_forward(k, slot, q, (1, 2))

    def row_leaf(k, *slots, also=True):
        for slot in slots:

            @pl.when((core != k) & row_wanted(k, slot) & also)
            def _():
                @pl.loop(0, CHUNKS)
                def _(q):
                    row_copy(k, slot, q, 0, 0).wait_recv()

    def swap_halves():
        return pltpu.make_async_remote_copy(
            src_ref=up.at[:, mine],
            dst_ref=up.at[:, mine],
            send_sem=swap_sem.at[0],
            recv_sem=swap_sem.at[1],
            device_id={"row": r + 1 - 2 * core},
            device_id_type=MESH,
        )

    def up_copy(k, source):
        return pltpu.make_async_remote_copy(
            src_ref=upper.at[k, :, mine],
            dst_ref=up.at[pl.ds(pl.multiple_of(source * up_rows, up_rows), up_rows), mine],
            send_sem=inv_send.at[0, k],
            recv_sem=up_recv.at[source],
            device_id={"col": k},
            device_id_type=MESH,
        )

    def low_copy(k, source):
        return pltpu.make_async_remote_copy(
            src_ref=lower.at[k],
            dst_ref=low.at[pl.ds(pl.multiple_of(source * low_rows, low_rows), low_rows)],
            send_sem=inv_send.at[1, k],
            recv_sem=low_recv.at[source],
            device_id={"row": k},
            device_id_type=MESH,
        )

    def lend_left():
        return pltpu.make_async_remote_copy(
            src_ref=ul.at[0, 0],
            dst_ref=colb.at[0, 0],
            send_sem=extra_sem.at[0],
            recv_sem=extra_sem.at[1],
            device_id={"col": 0},
            device_id_type=MESH,
        )

    def pass_mixed():
        return pltpu.make_async_remote_copy(
            src_ref=mix,
            dst_ref=mix,
            send_sem=extra_sem.at[2],
            recv_sem=extra_sem.at[3],
            device_id={"col": 1},
            device_id_type=MESH,
        )

    U, Y = 0, 1

    for a, b in every:
        fetch_left[a][b].wait()
        ul[a, b] = ul[a, b] * keep(a, b)
        if b == 0:
            for k in range(2):
                slot = col_slot(U, k, a)

                @pl.when((c == k) & col_wanted(k, slot))
                def _():
                    colb[k, slot] = ul[a, 0]

    for a, b in every:
        fetch_right[a][b].wait()
        out[a, b] = out[a, b] * keep(a, b)
        if a == 0:

            @pl.when(r == 0)
            def _():
                rowb[0, row_slot(Y, 0, b)] = out[0, b]

    pl.semaphore_wait(barrier, greeted)

    for k in range(2):

        @pl.when(c != k)
        def _():
            up_copy(k, c).start()

        @pl.when(r != k)
        def _():
            low_copy(k, r).start()

    def core_of(panel, a, b):
        return matmul_tn(
            colb[panel, col_slot(Y, panel, a)], rowb[panel, row_slot(U, panel, b)]
        ).astype(jnp.bfloat16)

    def subtract(panel, a, b, mixed):
        change = matmul_nt(rowb[panel, row_slot(Y, panel, b)], mixed)
        out[a, b] = (out[a, b].astype(jnp.float32) - change).astype(jnp.bfloat16)

    def update(panel, a, b, also=True):
        @pl.when((True if a > 0 else r > panel) & also)
        def _():
            meet = matmul_tn(ul[a, b], colb[panel, col_slot(U, panel, a)]).astype(jnp.bfloat16)
            mixed = matmul(meet, core_of(panel, a, b)).astype(jnp.bfloat16)
            subtract(panel, a, b, mixed)

    def wait_low(k):
        own_low(k).wait()
        for s in range(n_row):
            if s != k:
                low_copy(k, s).wait_recv()

    def solve_row(k, b, source=None):
        slot = row_slot(U, k, b)
        rowb[k, slot] = matmul(low[...], ul[0, b] if source is None else source[...]).astype(jnp.bfloat16)

    def solve_col(k, a):
        colb[k, col_slot(Y, k, a)] = matmul(up[...], out[a, 0]).astype(jnp.bfloat16)

    def share_row(b):
        rowb[1, row_slot(Y, 1, b)] = out[0, b]
        row_send_out(1, row_slot(Y, 1, b))

    even, odd = (r >= 2) & (core == 0), (r >= 2) & (core == 1)

    @pl.when(r == 0)
    def _():
        row_send_out(0, 0)
        row_send_out(0, 1)

    @pl.when(c < 2)
    def _():
        @pl.when((c == 1) & (r == 0))
        def _():
            lend_left().start()

        col_send_out(0, 0)
        col_send_out(1, 1, (1, 2))
        col_send_out(1, 0, (0,))
        col_send_out(1, 1, (0,))
        col_send_out(1, 0, (1, 2))

        @pl.when(r == 0)
        def _():
            wait_low(0)

            @pl.when(c == 0)
            def _():
                lend_left().wait_recv()
                solve_row(0, 0, colb.at[0, 0])

            @pl.when(c != 0)
            def _():
                solve_row(0, 0)

            row_send_out(0, 2)
            solve_row(0, 1)
            row_send_out(0, 3)

        for k in range(2):

            @pl.when(c == k)
            def _():
                own_up(k).wait()

        for s in range(n_col):

            @pl.when(s != c)
            def _():
                up_copy(0, s).wait_recv()

        swap_halves().start()
        swap_halves().wait_recv()

        @pl.when(c == 0)
        def _():
            @pl.when(r > 0)
            def _():
                solve_col(0, 0)

            col_send_out(0, 1)
            col_send_out(0, 2, (0,))
            solve_col(0, 1)
            col_send_out(0, 3, (0,))

        @pl.when(r == 1)
        def _():
            wait_low(1)
            solve_row(1, 1)
            row_send_out(1, 1)

        row_relay(0, even & (c == 1))
        row_relay(1, even)
        row_relay(2, even)
        row_leaf(0, 0, 2)

        @pl.when(c == 0)
        def _():
            col_leaf(1, 1)
            meet = matmul_tn(colb[1, col_slot(U, 1, 1)], ul[1, 0]).astype(jnp.bfloat16)
            mix[...] = matmul(meet, core_of(0, 1, 0)).astype(jnp.bfloat16)
            pass_mixed().start()
            col_send_out(0, 2, (1, 2))
            col_send_out(0, 3, (1, 2))

        @pl.when(c == 1)
        def _():
            col_leaf(0, 0, 1)
            update(0, 0, 0)

            @pl.when(r > 1)
            def _():
                solve_col(1, 0)

            col_send_out(1, 2)

        row_relay(3, even)
        row_leaf(0, 1, 3)
        update(0, 0, 1, also=r == 1)

        @pl.when(r == 1)
        def _():
            share_row(1)

        @pl.when(c == 1)
        def _():
            pass_mixed().wait_recv()
            subtract(0, 1, 0, mix[...])
            solve_col(1, 1)
            col_send_out(1, 3)

        row_relay(1, odd)
        update(0, 0, 1, also=r != 1)
        col_leaf(0, 2, 3)
        update(0, 1, 1)
        row_relay(3, odd)
        row_leaf(1, 1, 3)
        col_leaf(1, 0)
        col_leaf(1, 1, also=c != 0)
        col_leaf(1, 2)
        update(1, 0, 1)
        col_leaf(1, 3)
        update(1, 1, 1)
        for panel in range(2):
            for a in range(2):

                @pl.when((c == panel) & (True if a > 0 else r > panel))
                def _():
                    out[a, 0] = colb[panel, col_slot(Y, panel, a)]

    @pl.when((c >= 2) & (r < 2))
    def _():
        @pl.when(r == 0)
        def _():
            wait_low(0)
            for b in range(2):
                solve_row(0, b)
                row_send_out(0, 2 + b)

        col_relay(0, (r == 1) & (x == 0))
        col_relay(1, x == 1)
        col_relay(2, (r == 0) & (x == 0))

        @pl.when(r == 1)
        def _():
            wait_low(1)
            for b in range(2):
                solve_row(1, b)
                row_send_out(1, b)

            col_relay(1, x == 0)
            col_leaf(0, 0, 1)
            for b in range(2):
                row_leaf(0, b, 2 + b)
                update(0, 0, b)
                share_row(b)

            col_relay(2, x == 0)

        col_relay(3, x == 0)
        col_leaf(0, 2, 3)
        update(0, 1, 0)
        update(0, 1, 1)
        col_relay(3, x == 1)
        col_leaf(1, 1, 3)
        for b in range(2):
            row_leaf(1, b, 2 + b)
            update(1, 1, b)

    @pl.when((c >= 2) & (r >= 2))
    def _():
        main = x < 2

        def pump(slot, even_rows, odd_rows):
            @pl.loop(0, CHUNKS)
            def _(q):
                @pl.when(main)
                def _():
                    col_relay_piece(slot, q)

                for role, rows in ((core == 0, even_rows), (core == 1, odd_rows)):
                    for first, rate in rows:
                        for extra in range(rate):

                            @pl.when(role)
                            def _():
                                m = first * CHUNKS + q * rate + extra
                                row_relay_piece(m // CHUNKS, lax.rem(m, CHUNKS))

        pump(0, [(0, 1)], [])
        pump(1, [(1, 2)], [])
        col_leaf(0, 0, 1)
        row_leaf(0, 0, 2)
        update(0, 0, 0)
        pump(2, [(3, 1)], [(0, 2)])
        row_leaf(0, 1, 3)
        update(0, 0, 1)
        pump(3, [], [(2, 2)])
        col_leaf(1, 0, 2)
        for b in range(2):
            row_leaf(1, b, 2 + b)
            update(1, 0, b)
        col_leaf(0, 2, 3)
        update(0, 1, 0)
        update(0, 1, 1)
        col_leaf(1, 1, 3)
        update(1, 1, 0)
        update(1, 1, 1)

    for k in range(2):

        @pl.when(c != k)
        def _():
            up_copy(k, c).wait_send()

        @pl.when(r != k)
        def _():
            low_copy(k, r).wait_send()

    @pl.when(c < 2)
    def _():
        swap_halves().wait_send()

        @pl.when((c == 1) & (r == 0))
        def _():
            lend_left().wait_send()

        @pl.when(c == 0)
        def _():
            pass_mixed().wait_send()

    for k in range(2):
        for slot in range(4):
            for way, (needed, target) in enumerate(col_ways(k)):

                @pl.when(needed & col_wanted(k, slot))
                def _():
                    col_copy(k, slot, None, way, target).wait_send()

            for way, (needed, target) in enumerate(row_ways()):

                @pl.when((core == k) & needed & row_wanted(k, slot))
                def _():
                    row_copy(k, slot, None, way, target).wait_send()


def body(left, right, lower_inverse, upper_inverse, ranks):
    n_row, n_col = lax.axis_size("row"), lax.axis_size("col")
    minor_col = 4 if n_col % 4 == 0 and n_col > 8 else 2
    order, width = left.shape[2:]
    upper = jnp.swapaxes(upper_inverse, 1, 2)
    tile = (order, width)
    vmem = pl.BlockSpec(memory_space=pltpu.VMEM)
    hbm = pl.BlockSpec(memory_space=pltpu.HBM)
    return pl.pallas_call(
        functools.partial(kernel, n_row, n_col, minor_col),
        out_shape=jax.ShapeDtypeStruct(right.shape, jnp.bfloat16),
        in_specs=[pl.BlockSpec(memory_space=pltpu.SMEM)] + [hbm] * 4,
        out_specs=vmem,
        scratch_shapes=[
            pltpu.VMEM((2, 2) + tile, jnp.bfloat16),
            pltpu.VMEM((2, 4) + tile, jnp.bfloat16),
            pltpu.VMEM((2, 4) + tile, jnp.bfloat16),
            pltpu.VMEM((order, order), jnp.bfloat16),
            pltpu.VMEM((order, order), jnp.bfloat16),
            pltpu.VMEM((width, width), jnp.bfloat16),
            pltpu.SemaphoreType.DMA((2, 4, 3)),
            pltpu.SemaphoreType.DMA((2, 4, CHUNKS)),
            pltpu.SemaphoreType.DMA((2, 4, 2)),
            pltpu.SemaphoreType.DMA((2, 4, CHUNKS)),
            pltpu.SemaphoreType.DMA((2, 2)),
            pltpu.SemaphoreType.DMA((n_row,)),
            pltpu.SemaphoreType.DMA((n_col,)),
            pltpu.SemaphoreType.DMA((2, 2, 2)),
            pltpu.SemaphoreType.DMA((2,)),
            pltpu.SemaphoreType.DMA((4,)),
        ],
        compiler_params=pltpu.CompilerParams(
            collective_id=0, has_side_effects=True, vmem_limit_bytes=60 * 1024 * 1024
        ),
        cost_estimate=pl.CostEstimate(
            flops=2_000_000_000, bytes_accessed=4_000_000, transcendentals=0
        ),
    )(ranks, left, right, lower_inverse, upper)


def solution(mesh):
    placed = (
        P("row", "col", None, None),
        P("row", "col", None, None),
        P(None, "row", None),
        P(None, None, "col"),
        P("row", "col"),
    )
    return jax.shard_map(
        body, mesh=mesh, in_specs=placed, out_specs=P("row", "col", None, None), check_vma=False
    )
```

time: 53.4 us -> 51.2 us (0.959)
  the two profiles are of different devices: /device:TPU:28 before, /device:TPU:25 now
where the time goes in v2:
time: 51.2 us; the launch traced here: 51 us
  Pallas kernels  48.7 us (95%)
  local copies, waits for them, and re-layouts  2.26 us (4%)
    pallas_call x1, Pallas kernels, body(): pl.pallas_call(functools.partial(kernel, n_row, n_col, minor_col), out_sh...  48.7 us
    unnamed x1, local copies, waits for them, and re-layouts  2.26 us

profile of v2, /device:TPU:25, one launch (start us, length us, event | category | flops | bytes accessed | tf_op | source)
XLA Modules:
  0.0 51.0 jit_solution(10577956794067751813)
XLA Ops:
  0.0 48.7 %shard_map.55 = bf16[2,2,512,256]{3,2,1,0:T(8,128)(2,1)} custom-call(s32[2,2]{1,0:T(2,128)} %ranks.1, bf16[2,2,512,256]{3,2,1,0:T(8,128)(2,1)} %left.1, bf16[2,2,512,256]{3,2,1,0:T(8,128)(2,1)} %right.1, bf16[2,128,512]{2,1,0:T(8,128)(2,1)} %lower.1, bf16[2,64,512]{2,1,0:T(8,128)(2,1)} %bitcast.1), custom_call_target="tpu_custom_call" | custom-call | flops 2000000000 | bytes 4000000 | tf_op jit(solution)/shard_map/pallas_call | solution.py:590
  48.7 2.3 %copy.7 = bf16[2,2,512,256]{3,2,1,0:T(8,128)(2,1)} copy(bf16[2,2,512,256]{3,2,1,0:T(8,128)(2,1)} %shard_map.55) | data formatting | bytes 2097152

commit v3 on v2

--- a/solution.py
+++ b/solution.py
@@ -46,6 +46,10 @@
     for a, b in every:
         fetch_right[a][b].start()
 
+    @pl.when(c < 2)
+    def _():
+        up[...] = jnp.zeros_like(up)
+
     barrier = pltpu.get_barrier_semaphore()
 
     def greet(needed, **target):
@@ -83,9 +87,12 @@
             lower.at[k], low.at[pl.ds(k * low_rows, low_rows)], inv_send.at[1, k]
         )
 
+    def up_has(source):
+        return (source + 1) * up_rows > core * half
+
     for k in range(2):
 
-        @pl.when(c == k)
+        @pl.when((c == k) & up_has(k))
         def _():
             own_up(k).start()
 
@@ -293,11 +300,13 @@
 
     pl.semaphore_wait(barrier, greeted)
 
+    def give_up(k):
+        @pl.when((c != k) & up_has(c))
+        def _():
+            up_copy(k, c).start()
+
+    give_up(0)
     for k in range(2):
-
-        @pl.when(c != k)
-        def _():
-            up_copy(k, c).start()
 
         @pl.when(r != k)
         def _():
@@ -372,15 +381,16 @@
             solve_row(0, 1)
             row_send_out(0, 3)
 
+        give_up(1)
         for k in range(2):
 
-            @pl.when(c == k)
+            @pl.when((c == k) & up_has(k))
             def _():
                 own_up(k).wait()
 
         for s in range(n_col):
 
-            @pl.when(s != c)
+            @pl.when((s != c) & up_has(s))
             def _():
                 up_copy(0, s).wait_recv()
 
@@ -451,7 +461,6 @@
         row_relay(3, odd)
         row_leaf(1, 1, 3)
         col_leaf(1, 0)
-        col_leaf(1, 1, also=c != 0)
         col_leaf(1, 2)
         update(1, 0, 1)
         col_leaf(1, 3)
@@ -465,6 +474,8 @@
 
     @pl.when((c >= 2) & (r < 2))
     def _():
+        give_up(1)
+
         @pl.when(r == 0)
         def _():
             wait_low(0)
@@ -492,11 +503,10 @@
 
             col_relay(2, x == 0)
 
-        col_relay(3, x == 0)
+        col_relay(3, r >= 0)
         col_leaf(0, 2, 3)
         update(0, 1, 0)
         update(0, 1, 1)
-        col_relay(3, x == 1)
         col_leaf(1, 1, 3)
         for b in range(2):
             row_leaf(1, b, 2 + b)
@@ -506,8 +516,8 @@
     def _():
         main = x < 2
 
-        def pump(slot, even_rows, odd_rows):
-            @pl.loop(0, CHUNKS)
+        def pump(slot, even_rows, odd_rows, begin=0, end=CHUNKS):
+            @pl.loop(begin, end)
             def _(q):
                 @pl.when(main)
                 def _():
@@ -522,7 +532,9 @@
                                 m = first * CHUNKS + q * rate + extra
                                 row_relay_piece(m // CHUNKS, lax.rem(m, CHUNKS))
 
-        pump(0, [(0, 1)], [])
+        pump(0, [(0, 1)], [], end=CHUNKS // 4)
+        give_up(1)
+        pump(0, [(0, 1)], [], begin=CHUNKS // 4)
         pump(1, [(1, 2)], [])
         col_leaf(0, 0, 1)
         row_leaf(0, 0, 2)
@@ -544,7 +556,7 @@
 
     for k in range(2):
 
-        @pl.when(c != k)
+        @pl.when((c != k) & up_has(c))
         def _():
             up_copy(k, c).wait_send()
 

time: 51.2 us -> 46.9 us (0.916)
  the two profiles are of different devices: /device:TPU:25 before, /device:TPU:28 now
where the time goes in v3:
time: 46.9 us; the launch traced here: 46.4 us
  Pallas kernels  44.1 us (94%)
  local copies, waits for them, and re-layouts  2.26 us (5%)
    pallas_call x1, Pallas kernels, body(): pl.pallas_call(functools.partial(kernel, n_row, n_col, minor_col), out_sh...  44.1 us
    unnamed x1, local copies, waits for them, and re-layouts  2.26 us

profile of v3, /device:TPU:28, one launch (start us, length us, event | category | flops | bytes accessed | tf_op | source)
XLA Modules:
  0.0 46.4 jit_solution(18379985619336512594)
XLA Ops:
  0.0 44.1 %shard_map.55 = bf16[2,2,512,256]{3,2,1,0:T(8,128)(2,1)} custom-call(s32[2,2]{1,0:T(2,128)} %ranks.1, bf16[2,2,512,256]{3,2,1,0:T(8,128)(2,1)} %left.1, bf16[2,2,512,256]{3,2,1,0:T(8,128)(2,1)} %right.1, bf16[2,128,512]{2,1,0:T(8,128)(2,1)} %lower.1, bf16[2,64,512]{2,1,0:T(8,128)(2,1)} %bitcast.1), custom_call_target="tpu_custom_call" | custom-call | flops 2000000000 | bytes 4000000 | tf_op jit(solution)/shard_map/pallas_call | solution.py:602
  44.1 2.3 %copy.7 = bf16[2,2,512,256]{3,2,1,0:T(8,128)(2,1)} copy(bf16[2,2,512,256]{3,2,1,0:T(8,128)(2,1)} %shard_map.55) | data formatting | bytes 2097152

commit v4 on v3

--- a/solution.py
+++ b/solution.py
@@ -9,6 +9,8 @@
 
 CHUNKS = 8
 MESH = pl.DeviceIdType.MESH
+UP, ALONG = (0, 1, 2), (3, 4)
+ALL = UP + ALONG
 
 
 def matmul(a, b):
@@ -25,7 +27,7 @@
 
 def kernel(
     n_row, n_col, minor_col, ranks, left, right, lower, upper, out,
-    ul, colb, rowb, low, up, mix,
+    ul, colb, rowb, low, up, mix, part,
     col_send, col_recv, row_send, row_recv, inv_send, low_recv, up_recv, fetch_sem, swap_sem, extra_sem,
 ):
     r, c = lax.axis_index("row"), lax.axis_index("col")
@@ -60,7 +62,17 @@
     def count(*needed):
         return sum(flag.astype(jnp.int32) for flag in needed)
 
-    greet(c >= minor_col, col=c - minor_col)
+    depth = n_col // minor_col
+    z = lax.div(c, minor_col)
+    even_z = lax.rem(z, 2) == 0
+    if depth > 2:
+        skip, rise, fall = even_z & (z + 2 < depth), even_z & (z >= 2) & (z + 1 < depth), z == 2
+        greet(even_z & (z >= 2), col=c - 2 * minor_col)
+        greet(jnp.logical_not(even_z) & (z >= 3), col=c - minor_col)
+        greet(z == 1, col=c + minor_col)
+    else:
+        skip, rise, fall = z < 0, z + 1 < depth, z < 0
+        greet(z >= 1, col=c - minor_col)
     greet(r >= 2, row=r - 2)
     greet(r >= 0, row=r + 1 - 2 * core)
     greet(x + 1 < minor_col, col=c + 1)
@@ -70,7 +82,7 @@
     for d in range(1, n_col):
         greet(c < 2, col=lax.rem(c + d, n_col))
     greeted = 1 + count(
-        r + 2 < n_row, x + 1 < minor_col, x >= 1, c + minor_col < n_col, r != 0, r != 1, c != 0, c != 1
+        r + 2 < n_row, x + 1 < minor_col, x >= 1, skip, rise, fall, r != 0, r != 1, c != 0, c != 1
     )
 
     half = order // 2
@@ -145,7 +157,9 @@
 
     def col_ways(k):
         return [
-            ((x == k) & (c + minor_col < n_col), c + minor_col),
+            ((x == k) & skip, c + 2 * minor_col),
+            ((x == k) & rise, c + minor_col),
+            ((x == k) & fall, c - minor_col),
             ((x >= k) & (x + 1 < minor_col), c + 1),
             ((x <= k) & (x >= 1), c - 1),
         ]
@@ -153,7 +167,7 @@
     def row_ways():
         return [(r + 2 < n_row, r + 2), (r >= 0, r + 1 - 2 * core)]
 
-    def col_forward(k, slot, q, ways=(0, 1, 2)):
+    def col_forward(k, slot, q, ways=ALL):
         for way in ways:
             needed, target = col_ways(k)[way]
 
@@ -168,7 +182,7 @@
             def _():
                 row_copy(k, slot, q, way, target).start()
 
-    def col_send_out(k, slot, ways=(0, 1, 2)):
+    def col_send_out(k, slot, ways=ALL):
         @pl.when((c == k) & col_wanted(k, slot))
         def _():
             @pl.loop(0, CHUNKS)
@@ -215,7 +229,7 @@
                 def _(q):
                     col_copy(k, slot, q, 0, 0).wait_recv()
                     if minor_col > 2:
-                        col_forward(k, slot, q, (1, 2))
+                        col_forward(k, slot, q, ALONG)
 
     def row_leaf(k, *slots, also=True):
         for slot in slots:
@@ -317,6 +331,9 @@
             colb[panel, col_slot(Y, panel, a)], rowb[panel, row_slot(U, panel, b)]
         ).astype(jnp.bfloat16)
 
+    def meet_of(panel, a, b):
+        return matmul_tn(ul[a, b], colb[panel, col_slot(U, panel, a)]).astype(jnp.bfloat16)
+
     def subtract(panel, a, b, mixed):
         change = matmul_nt(rowb[panel, row_slot(Y, panel, b)], mixed)
         out[a, b] = (out[a, b].astype(jnp.float32) - change).astype(jnp.bfloat16)
@@ -324,9 +341,17 @@
     def update(panel, a, b, also=True):
         @pl.when((True if a > 0 else r > panel) & also)
         def _():
-            meet = matmul_tn(ul[a, b], colb[panel, col_slot(U, panel, a)]).astype(jnp.bfloat16)
-            mixed = matmul(meet, core_of(panel, a, b)).astype(jnp.bfloat16)
+            mixed = matmul(meet_of(panel, a, b), core_of(panel, a, b)).astype(jnp.bfloat16)
             subtract(panel, a, b, mixed)
+
+    def meet(panel, a, b):
+        part[panel, a, b] = meet_of(panel, a, b)
+
+    def blend(panel, a, b):
+        part[panel, a, b] = matmul(part[panel, a, b], core_of(panel, a, b)).astype(jnp.bfloat16)
+
+    def apply(panel, a, b):
+        subtract(panel, a, b, part[panel, a, b])
 
     def wait_low(k):
         own_low(k).wait()
@@ -359,10 +384,10 @@
             lend_left().start()
 
         col_send_out(0, 0)
-        col_send_out(1, 1, (1, 2))
-        col_send_out(1, 0, (0,))
-        col_send_out(1, 1, (0,))
-        col_send_out(1, 0, (1, 2))
+        col_send_out(1, 1, ALONG)
+        col_send_out(1, 0, UP)
+        col_send_out(1, 1, UP)
+        col_send_out(1, 0, ALONG)
 
         @pl.when(r == 0)
         def _():
@@ -404,9 +429,9 @@
                 solve_col(0, 0)
 
             col_send_out(0, 1)
-            col_send_out(0, 2, (0,))
+            col_send_out(0, 2, UP)
             solve_col(0, 1)
-            col_send_out(0, 3, (0,))
+            col_send_out(0, 3, UP)
 
         @pl.when(r == 1)
         def _():
@@ -422,11 +447,11 @@
         @pl.when(c == 0)
         def _():
             col_leaf(1, 1)
-            meet = matmul_tn(colb[1, col_slot(U, 1, 1)], ul[1, 0]).astype(jnp.bfloat16)
-            mix[...] = matmul(meet, core_of(0, 1, 0)).astype(jnp.bfloat16)
+            crossed = matmul_tn(colb[1, col_slot(U, 1, 1)], ul[1, 0]).astype(jnp.bfloat16)
+            mix[...] = matmul(crossed, core_of(0, 1, 0)).astype(jnp.bfloat16)
             pass_mixed().start()
-            col_send_out(0, 2, (1, 2))
-            col_send_out(0, 3, (1, 2))
+            col_send_out(0, 2, ALONG)
+            col_send_out(0, 3, ALONG)
 
         @pl.when(c == 1)
         def _():
@@ -503,14 +528,22 @@
 
             col_relay(2, x == 0)
 
-        col_relay(3, r >= 0)
-        col_leaf(0, 2, 3)
-        update(0, 1, 0)
-        update(0, 1, 1)
-        col_leaf(1, 1, 3)
+        col_relay(3, x == 0)
+        col_leaf(0, 2)
+        col_leaf(1, 1)
+        for panel in range(2):
+            for b in range(2):
+                meet(panel, 1, b)
+        col_relay(3, x == 1)
+        col_leaf(0, 3)
         for b in range(2):
-            row_leaf(1, b, 2 + b)
-            update(1, 1, b)
+            blend(0, 1, b)
+            apply(0, 1, b)
+        row_leaf(1, 0, 1, 2, 3)
+        col_leaf(1, 3)
+        for b in range(2):
+            blend(1, 1, b)
+            apply(1, 1, b)
 
     @pl.when((c >= 2) & (r >= 2))
     def _():
@@ -535,24 +568,72 @@
         pump(0, [(0, 1)], [], end=CHUNKS // 4)
         give_up(1)
         pump(0, [(0, 1)], [], begin=CHUNKS // 4)
+        def pump_beside(slot, even_rows, odd_rows, jobs):
+            for q in range(CHUNKS):
+                pump(slot, even_rows, odd_rows, q, q + 1)
+                if q < len(jobs) and jobs[q] is not None:
+                    jobs[q]()
+
+        def last_meet():
+            col_leaf(0, 2)
+            meet(0, 1, 0)
+
+        def next_blend():
+            col_leaf(1, 2)
+            row_leaf(1, 0)
+            blend(1, 0, 0)
+
+        def last_blend():
+            row_leaf(1, 1)
+            blend(1, 0, 1)
+
         pump(1, [(1, 2)], [])
         col_leaf(0, 0, 1)
         row_leaf(0, 0, 2)
-        update(0, 0, 0)
-        pump(2, [(3, 1)], [(0, 2)])
+        col_leaf(1, 0, 1)
+        at = functools.partial
+        pump_beside(
+            2,
+            [(3, 1)],
+            [(0, 2)],
+            [
+                at(meet, 0, 0, 0),
+                at(blend, 0, 0, 0),
+                at(apply, 0, 0, 0),
+                at(meet, 0, 0, 1),
+                at(meet, 1, 0, 0),
+                at(meet, 1, 0, 1),
+                at(meet, 1, 1, 0),
+                at(meet, 1, 1, 1),
+            ],
+        )
         row_leaf(0, 1, 3)
-        update(0, 0, 1)
-        pump(3, [], [(2, 2)])
-        col_leaf(1, 0, 2)
+        pump_beside(
+            3,
+            [],
+            [(2, 2)],
+            [
+                at(blend, 0, 0, 1),
+                at(apply, 0, 0, 1),
+                None,
+                last_meet,
+                at(meet, 0, 1, 1),
+                None,
+                next_blend,
+                last_blend,
+            ],
+        )
         for b in range(2):
-            row_leaf(1, b, 2 + b)
-            update(1, 0, b)
-        col_leaf(0, 2, 3)
-        update(0, 1, 0)
-        update(0, 1, 1)
-        col_leaf(1, 1, 3)
-        update(1, 1, 0)
-        update(1, 1, 1)
+            row_leaf(1, 2 + b)
+            apply(1, 0, b)
+        col_leaf(0, 3)
+        for b in range(2):
+            blend(0, 1, b)
+            apply(0, 1, b)
+        col_leaf(1, 3)
+        for b in range(2):
+            blend(1, 1, b)
+            apply(1, 1, b)
 
     for k in range(2):
 
@@ -601,7 +682,7 @@
     hbm = pl.BlockSpec(memory_space=pltpu.HBM)
     return pl.pallas_call(
         functools.partial(kernel, n_row, n_col, minor_col),
-        out_shape=jax.ShapeDtypeStruct(right.shape, jnp.bfloat16),
+        out_shape=pltpu.VMEM(right.shape, jnp.bfloat16),
         in_specs=[pl.BlockSpec(memory_space=pltpu.SMEM)] + [hbm] * 4,
         out_specs=vmem,
         scratch_shapes=[
@@ -611,7 +692,8 @@
             pltpu.VMEM((order, order), jnp.bfloat16),
             pltpu.VMEM((order, order), jnp.bfloat16),
             pltpu.VMEM((width, width), jnp.bfloat16),
-            pltpu.SemaphoreType.DMA((2, 4, 3)),
+            pltpu.VMEM((2, 2, 2, width, width), jnp.bfloat16),
+            pltpu.SemaphoreType.DMA((2, 4, 5)),
             pltpu.SemaphoreType.DMA((2, 4, CHUNKS)),
             pltpu.SemaphoreType.DMA((2, 4, 2)),
             pltpu.SemaphoreType.DMA((2, 4, CHUNKS)),

time: 46.9 us -> 43.7 us (0.932)
  the two profiles are of different devices: /device:TPU:28 before, /device:TPU:13 now
where the time goes in v4:
time: 43.7 us; the launch traced here: 43.5 us
  Pallas kernels  42.5 us (97%)
  local copies, waits for them, and re-layouts  0.97 us (2%)
    pallas_call x1, Pallas kernels, body(): pl.pallas_call(functools.partial(kernel, n_row, n_col, minor_col), out_sh...  42.5 us
    unnamed x1, local copies, waits for them, and re-layouts  0.97 us

profile of v4, /device:TPU:13, one launch (start us, length us, event | category | flops | bytes accessed | tf_op | source)
XLA Modules:
  0.0 43.5 jit_solution(4315294986587449259)
XLA Ops:
  0.0 42.5 %shard_map.55 = bf16[2,2,512,256]{3,2,1,0:T(8,128)(2,1)S(1)} custom-call(s32[2,2]{1,0:T(2,128)} %ranks.1, bf16[2,2,512,256]{3,2,1,0:T(8,128)(2,1)} %left.1, bf16[2,2,512,256]{3,2,1,0:T(8,128)(2,1)} %right.1, bf16[2,128,512]{2,1,0:T(8,128)(2,1)} %lower.1, bf16[2,64,512]{2,1,0:T(8,128)(2,1)} %bitcast.1), custom_call_target="tpu_custom_call" | custom-call | flops 2000000000 | bytes 4000000 | tf_op jit(solution)/shard_map/pallas_call | solution.py:683
  42.5 1.0 %copy.7 = bf16[2,2,512,256]{3,2,1,0:T(8,128)(2,1)} copy(bf16[2,2,512,256]{3,2,1,0:T(8,128)(2,1)S(1)} %shard_map.55) | data formatting | bytes 2097152

commit v5 on v4

--- a/solution.py
+++ b/solution.py
@@ -42,12 +42,6 @@
         [pltpu.make_async_copy(right.at[a, b], out.at[a, b], fetch_sem.at[1, a, b]) for b in range(2)]
         for a in range(2)
     ]
-    every = [(0, 0), (1, 0), (0, 1), (1, 1)]
-    for a, b in every:
-        fetch_left[a][b].start()
-    for a, b in every:
-        fetch_right[a][b].start()
-
     @pl.when(c < 2)
     def _():
         up[...] = jnp.zeros_like(up)
@@ -62,6 +56,10 @@
     def count(*needed):
         return sum(flag.astype(jnp.int32) for flag in needed)
 
+    for d in range(n_col - 1, 0, -1):
+        greet(c < 2, col=lax.rem(c + d, n_col))
+    for d in range(1, n_row):
+        greet(r < 2, row=lax.rem(r + d, n_row))
     depth = n_col // minor_col
     z = lax.div(c, minor_col)
     even_z = lax.rem(z, 2) == 0
@@ -77,13 +75,18 @@
     greet(r >= 0, row=r + 1 - 2 * core)
     greet(x + 1 < minor_col, col=c + 1)
     greet(x >= 1, col=c - 1)
-    for d in range(1, n_row):
-        greet(r < 2, row=lax.rem(r + d, n_row))
-    for d in range(1, n_col):
-        greet(c < 2, col=lax.rem(c + d, n_col))
     greeted = 1 + count(
         r + 2 < n_row, x + 1 < minor_col, x >= 1, skip, rise, fall, r != 0, r != 1, c != 0, c != 1
     )
+
+    for a in range(2):
+        fetch_left[a][0].start()
+    for b in range(2):
+        fetch_right[0][b].start()
+    for a in range(2):
+        fetch_left[a][1].start()
+    for b in range(2):
+        fetch_right[1][b].start()
 
     half = order // 2
     mine = pl.ds(pl.multiple_of(core * half, half), half)
@@ -292,25 +295,29 @@
 
     U, Y = 0, 1
 
-    for a, b in every:
+    def take_left(a, b):
         fetch_left[a][b].wait()
         ul[a, b] = ul[a, b] * keep(a, b)
-        if b == 0:
-            for k in range(2):
-                slot = col_slot(U, k, a)
-
-                @pl.when((c == k) & col_wanted(k, slot))
-                def _():
-                    colb[k, slot] = ul[a, 0]
-
-    for a, b in every:
+
+    def take_right(a, b):
         fetch_right[a][b].wait()
         out[a, b] = out[a, b] * keep(a, b)
-        if a == 0:
-
-            @pl.when(r == 0)
-            def _():
-                rowb[0, row_slot(Y, 0, b)] = out[0, b]
+
+    for a in range(2):
+        take_left(a, 0)
+        for k in range(2):
+            slot = col_slot(U, k, a)
+
+            @pl.when((c == k) & col_wanted(k, slot))
+            def _():
+                colb[k, slot] = ul[a, 0]
+
+    for b in range(2):
+        take_right(0, b)
+
+        @pl.when(r == 0)
+        def _():
+            rowb[0, row_slot(Y, 0, b)] = out[0, b]
 
     pl.semaphore_wait(barrier, greeted)
 
@@ -389,6 +396,13 @@
         col_send_out(1, 1, UP)
         col_send_out(1, 0, ALONG)
 
+    for t in range(2):
+        take_left(t, 1)
+    for t in range(2):
+        take_right(1, t)
+
+    @pl.when(c < 2)
+    def _():
         @pl.when(r == 0)
         def _():
             wait_low(0)
@@ -528,13 +542,12 @@
 
             col_relay(2, x == 0)
 
-        col_relay(3, x == 0)
+        col_relay(3, r >= 0)
         col_leaf(0, 2)
         col_leaf(1, 1)
         for panel in range(2):
             for b in range(2):
                 meet(panel, 1, b)
-        col_relay(3, x == 1)
         col_leaf(0, 3)
         for b in range(2):
             blend(0, 1, b)
@@ -565,9 +578,8 @@
                                 m = first * CHUNKS + q * rate + extra
                                 row_relay_piece(m // CHUNKS, lax.rem(m, CHUNKS))
 
-        pump(0, [(0, 1)], [], end=CHUNKS // 4)
         give_up(1)
-        pump(0, [(0, 1)], [], begin=CHUNKS // 4)
+        pump(0, [(0, 1)], [])
         def pump_beside(slot, even_rows, odd_rows, jobs):
             for q in range(CHUNKS):
                 pump(slot, even_rows, odd_rows, q, q + 1)
@@ -611,7 +623,7 @@
         pump_beside(
             3,
             [],
-            [(2, 2)],
+            [],
             [
                 at(blend, 0, 0, 1),
                 at(apply, 0, 0, 1),
@@ -624,6 +636,7 @@
             ],
         )
         for b in range(2):
+            row_relay(2 + b, core == 1)
             row_leaf(1, 2 + b)
             apply(1, 0, b)
         col_leaf(0, 3)

time: 43.7 us -> 42.8 us (0.979)
  the two profiles are of different devices: /device:TPU:13 before, /device:TPU:14 now
where the time goes in v5:
time: 42.8 us; the launch traced here: 42.6 us
  Pallas kernels  41.6 us (97%)
  local copies, waits for them, and re-layouts  0.97 us (2%)
    pallas_call x1, Pallas kernels, body(): pl.pallas_call(functools.partial(kernel, n_row, n_col, minor_col), out_sh...  41.6 us
    unnamed x1, local copies, waits for them, and re-layouts  0.97 us

profile of v5, /device:TPU:14, one launch (start us, length us, event | category | flops | bytes accessed | tf_op | source)
XLA Modules:
  0.0 42.6 jit_solution(207263458595166352)
XLA Ops:
  0.0 41.6 %shard_map.55 = bf16[2,2,512,256]{3,2,1,0:T(8,128)(2,1)S(1)} custom-call(s32[2,2]{1,0:T(2,128)} %ranks.1, bf16[2,2,512,256]{3,2,1,0:T(8,128)(2,1)} %left.1, bf16[2,2,512,256]{3,2,1,0:T(8,128)(2,1)} %right.1, bf16[2,128,512]{2,1,0:T(8,128)(2,1)} %lower.1, bf16[2,64,512]{2,1,0:T(8,128)(2,1)} %bitcast.1), custom_call_target="tpu_custom_call" | custom-call | flops 2000000000 | bytes 4000000 | tf_op jit(solution)/shard_map/pallas_call | solution.py:696
  41.6 1.0 %copy.7 = bf16[2,2,512,256]{3,2,1,0:T(8,128)(2,1)} copy(bf16[2,2,512,256]{3,2,1,0:T(8,128)(2,1)S(1)} %shard_map.55) | data formatting | bytes 2097152

commit v6 on v5

--- a/solution.py
+++ b/solution.py
@@ -357,6 +357,13 @@
     def blend(panel, a, b):
         part[panel, a, b] = matmul(part[panel, a, b], core_of(panel, a, b)).astype(jnp.bfloat16)
 
+    def finish(panel, a):
+        mixed = [
+            matmul(part[panel, a, b], core_of(panel, a, b)).astype(jnp.bfloat16) for b in range(2)
+        ]
+        for b in range(2):
+            subtract(panel, a, b, mixed[b])
+
     def apply(panel, a, b):
         subtract(panel, a, b, part[panel, a, b])
 
@@ -549,14 +556,10 @@
             for b in range(2):
                 meet(panel, 1, b)
         col_leaf(0, 3)
-        for b in range(2):
-            blend(0, 1, b)
-            apply(0, 1, b)
+        finish(0, 1)
         row_leaf(1, 0, 1, 2, 3)
         col_leaf(1, 3)
-        for b in range(2):
-            blend(1, 1, b)
-            apply(1, 1, b)
+        finish(1, 1)
 
     @pl.when((c >= 2) & (r >= 2))
     def _():
@@ -637,16 +640,13 @@
         )
         for b in range(2):
             row_relay(2 + b, core == 1)
-            row_leaf(1, 2 + b)
+        row_leaf(1, 2, 3)
+        for b in range(2):
             apply(1, 0, b)
         col_leaf(0, 3)
-        for b in range(2):
-            blend(0, 1, b)
-            apply(0, 1, b)
+        finish(0, 1)
         col_leaf(1, 3)
-        for b in range(2):
-            blend(1, 1, b)
-            apply(1, 1, b)
+        finish(1, 1)
 
     for k in range(2):
 

time: 42.8 us -> 42.6 us (level)
  no operation moved by 1% of the time
where the time goes in v6:
time: 42.6 us; the launch traced here: 42.5 us
  Pallas kernels  41.5 us (97%)
  local copies, waits for them, and re-layouts  0.97 us (2%)
    pallas_call x1, Pallas kernels, body(): pl.pallas_call(functools.partial(kernel, n_row, n_col, minor_col), out_sh...  41.5 us
    unnamed x1, local copies, waits for them, and re-layouts  0.97 us

profile of v6, /device:TPU:14, one launch (start us, length us, event | category | flops | bytes accessed | tf_op | source)
XLA Modules:
  0.0 42.5 jit_solution(13187106630262405796)
XLA Ops:
  0.0 41.5 %shard_map.55 = bf16[2,2,512,256]{3,2,1,0:T(8,128)(2,1)S(1)} custom-call(s32[2,2]{1,0:T(2,128)} %ranks.1, bf16[2,2,512,256]{3,2,1,0:T(8,128)(2,1)} %left.1, bf16[2,2,512,256]{3,2,1,0:T(8,128)(2,1)} %right.1, bf16[2,128,512]{2,1,0:T(8,128)(2,1)} %lower.1, bf16[2,64,512]{2,1,0:T(8,128)(2,1)} %bitcast.1), custom_call_target="tpu_custom_call" | custom-call | flops 2000000000 | bytes 4000000 | tf_op jit(solution)/shard_map/pallas_call | solution.py:696
  41.5 1.0 %copy.7 = bf16[2,2,512,256]{3,2,1,0:T(8,128)(2,1)} copy(bf16[2,2,512,256]{3,2,1,0:T(8,128)(2,1)S(1)} %shard_map.55) | data formatting | bytes 2097152
